TPU v7x, 32 devices: a whole 2x2x4 slice. The times are simulated.
32 devices in a mesh: grp: 2 (over y), tp: 4 (over z), pp: 2 (over x), rep: 2 (over core).
Axes of the slice: x: 2, y: 2, z: 4, core: 2. Of those that a mesh axis runs over, the one named last changes fastest.
Arguments:
- first_tokens: bfloat16 [32, 14336], P('grp', 'tp'), parts along dimension 0, may hold values from -6 to 6
- second_tokens: bfloat16 [32, 14336], P('grp', 'tp'), parts along dimension 0, may hold values from -6 to 6
- qkv_weight: bfloat16 [14336, 3, 64, 128], P('tp', None, ('pp', 'rep')), may hold values from -0.046875 to 0.046875
- cache: bfloat16 [32, 64, 2, 64, 128], P(('grp', 'tp'), None, None, ('pp', 'rep')), parts along dimension 0, may hold values from -6 to 6
- lengths: int32 [32], P('grp'), parts along dimension 0, may hold values from 1 to 62, 496 in all
- matching: int32 [8], P('grp'), parts along dimension 0, may hold values from 0 to 3, as said below
Outputs:
- attended: bfloat16 [2, 32, 8192], P(None, ('grp', 'tp'), ('pp', 'rep')), parts along dimension 1
- new_cache: bfloat16 [32, 64, 2, 64, 128], P(('grp', 'tp'), None, None, ('pp', 'rep')), parts along dimension 0
There are 2 independent parts, one for each index of `grp`. A program takes and returns all parts, laid end to end along the dimension named above; an argument that names none is the same for every part. Nothing has to cross between parts.
Inputs may be any that keep to these rules, and one draw needn't show every extreme that they name: matching[t] = (t + matching[0]) mod 4 for every t: all old owners move by one common offset.
All inputs are finite; a program needn't handle non-finite values.
Results may differ from a plain program's by a relative error of at most 0.012.
Values may be sent and summed in bfloat16 or wider, within the bound.
No kernel may reach another device: no remote copies, remote signals or barrier semaphores. Data moves between devices by JAX's collectives and lax.ppermute only.
A program may use at most 128 MiB of HBM per device.

v0:
```python
import functools
import math

import jax
import jax.numpy as jnp
from jax import lax
from jax.experimental import pallas as pl
from jax.experimental.pallas import tpu as pltpu
from jax.sharding import PartitionSpec as P

WIDEST_SWITCH = 8


def shifted(block, axis, by):
    devices = lax.axis_size(axis)
    return lax.ppermute(block, axis, [(i, (i + by) % devices) for i in range(devices)])


def rotate_by_bits(block, offset, owners):
    for level in range((owners - 1).bit_length()):
        moved = shifted(block, "tp", 1 << level)
        block = jnp.where(offset >> level & 1 == 1, moved, block)
    return block


def owner_order(owners):
    order = [0]
    for level in reversed(range((owners - 1).bit_length())):
        order = order + [i ^ (1 << level) for i in order]
    return order


def reduce_by_halves(parts, owners):
    order = owner_order(owners)
    for level in range((owners - 1).bit_length()):
        half = parts.shape[0] // 2
        kept, sent = parts[:half], parts[half:].astype(jnp.bfloat16)
        assert all(order[half + j] == order[j] ^ (1 << level) for j in range(half))
        got = lax.ppermute(sent, "tp", [(i, i ^ (1 << level)) for i in range(owners)])
        parts = kept + got.astype(jnp.float32)
        order = order[:half]
    return parts[0]


def reduce_at_once(parts, owners):
    total = parts[0]
    for distance in range(1, owners):
        block = parts[owner_order(owners).index(distance)].astype(jnp.bfloat16)
        got = lax.ppermute(block, "tp", [(i, i ^ distance) for i in range(owners)])
        total = total + got.astype(jnp.float32)
    return total


def attention_kernel(
    lengths_ref, matching_ref, fresh_ref, cache_ref, moved_ref, attended_ref, filled_ref, block, mixed, result, in_sems, out_sems, result_sem
):
    rows, spots, _, heads, head_dim = block.shape
    steps = fresh_ref.shape[0]
    stays = matching_ref[0] == 0
    loads = [pltpu.make_async_copy(moved_ref.at[r], block.at[r], in_sems.at[r]) for r in range(rows)]
    for r in range(rows):

        @pl.when(stays)
        def _(r=r):
            pltpu.make_async_copy(cache_ref.at[r], block.at[r], in_sems.at[r]).start()

        @pl.when(jnp.logical_not(stays))
        def _(r=r):
            loads[r].start()

    owners = lax.axis_size("tp")
    first_row = lax.rem(lax.axis_index("tp") - matching_ref[0] + owners, owners) * rows
    first_head = lax.axis_index(("pp", "rep")) * heads
    shape = (spots * heads, steps * heads)
    row, column = (lax.broadcasted_iota(jnp.int32, shape, axis) for axis in range(2))
    spot, step = row // heads, column // heads
    own = row % heads == column % heads
    head = (first_head + 1 + column % heads).astype(jnp.float32)
    slopes = jnp.exp(head * (-math.log(2.0) / 8.0))
    since = (step - spot).astype(jnp.float32)
    allowed = jnp.where(own, step - spot, -2 * spots)
    stores = []
    for r in range(rows):
        loads[r].wait()
        at = lengths_ref[first_row + r]
        for s in range(steps):
            for part in range(2):
                block[r, at + s, part] = fresh_ref[s, r, 1 + part]
        stores.append(pltpu.make_async_copy(block.at[r], filled_ref.at[r], out_sems.at[r]))
        stores[-1].start()
        keys = block[r, :, 0].reshape(spots * heads, head_dim)
        values = block[r, :, 1].reshape(spots * heads, head_dim)
        query = fresh_ref[:, r, 0].reshape(steps * heads, head_dim)
        scores = lax.dot_general(keys, query, (((1,), (1,)), ((), ())), preferred_element_type=jnp.float32)
        scores = scores * head_dim ** (-0.5) - slopes * (since + at.astype(jnp.float32))
        scores = jnp.where(allowed + at >= 0, scores, -1e30)
        weights = jnp.exp(scores - jnp.max(scores, axis=0, keepdims=True)).astype(values.dtype)
        sums = lax.dot_general(
            weights, jnp.ones_like(values), (((0,), (0,)), ((), ())), preferred_element_type=jnp.float32
        )
        mix = lax.dot_general(weights, values, (((0,), (0,)), ((), ())), preferred_element_type=jnp.float32)
        mixed[:, r] = (mix / sums).reshape(steps, heads, head_dim)
    for s in range(steps):
        for h in range(heads):
            result[s, :, h * head_dim : (h + 1) * head_dim] = mixed[s, :, h].astype(result.dtype)
    finish = pltpu.make_async_copy(result, attended_ref, result_sem)
    finish.start()
    for store in stores:
        store.wait()
    finish.wait()


def unwritten(like):
    return pl.pallas_call(
        lambda out_ref: None,
        out_shape=jax.ShapeDtypeStruct(like.shape, like.dtype),
        out_specs=pl.BlockSpec(memory_space=pl.ANY),
        name="unwritten",
    )()


def attend_and_write(cache, moved, fresh, lengths, matching):
    rows, _, _, heads, head_dim = cache.shape
    steps = fresh.shape[0]
    smem = pl.BlockSpec(memory_space=pltpu.SMEM)
    anywhere = pl.BlockSpec(memory_space=pl.ANY)
    attended = jax.ShapeDtypeStruct((steps, rows, heads * head_dim), jnp.bfloat16)
    return pl.pallas_call(
        attention_kernel,
        out_shape=(attended, jax.ShapeDtypeStruct(cache.shape, cache.dtype)),
        in_specs=[smem, smem, pl.BlockSpec(memory_space=pltpu.VMEM), anywhere, anywhere],
        out_specs=(anywhere, anywhere),
        scratch_shapes=[
            pltpu.VMEM(cache.shape, cache.dtype),
            pltpu.VMEM((steps, rows, heads, head_dim), jnp.float32),
            pltpu.VMEM(attended.shape, attended.dtype),
            pltpu.SemaphoreType.DMA((rows,)),
            pltpu.SemaphoreType.DMA((rows,)),
            pltpu.SemaphoreType.DMA,
        ],
        compiler_params=pltpu.CompilerParams(vmem_limit_bytes=32 << 20),
        cost_estimate=pl.CostEstimate(flops=0, bytes_accessed=4 * cache.size, transcendentals=0),
        name="attend",
    )(lengths, matching, fresh, cache, moved)


def order_tokens(token_arrays, owners, local_rows):
    rank = lax.axis_index("tp")
    blocks = [tokens.reshape(owners, local_rows, -1) for tokens in token_arrays]
    return jnp.concatenate(
        [
            lax.dynamic_index_in_dim(block, rank ^ distance, 0, keepdims=False)
            for distance in owner_order(owners)
            for block in blocks
        ]
    )


def shards(first_tokens, second_tokens, qkv_weight, cache, lengths, matching):
    owners = lax.axis_size("tp")
    assert owners & (owners - 1) == 0
    local_rows = cache.shape[0]
    heads_local = qkv_weight.shape[2]
    head_dim = qkv_weight.shape[3]
    offset = matching[0]

    def serve(move, reduce, first_tokens, second_tokens, qkv_weight, cache):
        moved = move(cache)
        tokens = order_tokens((first_tokens, second_tokens), owners, local_rows)
        parts = jnp.dot(tokens, qkv_weight.reshape(qkv_weight.shape[0], -1), preferred_element_type=jnp.float32)
        total = reduce(parts.reshape(owners, 2 * local_rows, -1), owners)
        fresh = total.astype(jnp.bfloat16).reshape(2, local_rows, 3, heads_local, head_dim)
        return moved, fresh

    args = (first_tokens, second_tokens, qkv_weight, cache)
    if owners > WIDEST_SWITCH:
        moved = serve(lambda block: rotate_by_bits(block, offset, owners), reduce_by_halves, *args)
    else:
        branches = []
        for by in range(owners):
            hops = min(by, owners - by)
            move = functools.partial(shifted, axis="tp", by=by) if by else unwritten
            branches.append(functools.partial(serve, move, reduce_by_halves if hops > 1 else reduce_at_once))
        moved = lax.switch(offset, branches, *args)
    return attend_and_write(cache, *moved, lengths, matching)


def solution(mesh):
    in_specs = (
        P("grp", "tp"),
        P("grp", "tp"),
        P("tp", None, ("pp", "rep"), None),
        P(("grp", "tp"), None, None, ("pp", "rep"), None),
        P("grp"),
        P("grp"),
    )
    out_specs = (
        P(None, ("grp", "tp"), ("pp", "rep")),
        P(("grp", "tp"), None, None, ("pp", "rep"), None),
    )
    return jax.shard_map(shards, mesh=mesh, in_specs=in_specs, out_specs=out_specs, check_vma=False)
```

profile of v0, /device:TPU:0, one launch (start us, length us, event | category | flops | bytes accessed | tf_op | source)
XLA Modules:
  0.0 106.0 jit_solution(1801006561164840389)
XLA Ops:
  1.3 0.0 copy-start
  1.3 0.0 copy-start.1
  1.3 99.7 %conditional.1 = (bf16[4,64,2,16,128]{4,3,2,1,0:T(8,128)(2,1)}, bf16[2,4,3,16,128]{4,3,2,1,0:T(8,128)(2,1)S(1)}) conditional(s32[]{:T(128)} %bitcast.34, (bf16[16,3584]{1,0:T(8,128)(2,1)}, bf16[16,3584]{1,0:T(8,128)(2,1)}, bf16[3584,3,16,128]{3,2,1,0:T(8,128)(2,1)}) %tuple.23, ...), branch_computations={%region_0.1_spmd, %region_1.2_spmd, %region_2.3_spmd, %region_3.4_... | conditional | flops 1409826816 | bytes 58163556 | solution.py:184
  1.5 4.1 %collective-permute-start.7 = (bf16[4,64,2,16,128]{4,3,2,1,0:T(8,128)(2,1)}, bf16[4,64,2,16,128]{4,3,2,1,0:T(8,128)(2,1)}, u32[]{:S(2)}, u32[]{:S(2)}) collective-permute-start(bf16[4,64,2,16,128]{4,3,2,1,0:T(8,128)(2,1)} %get-tuple-element.37), channel_id=1, source_target_pairs={{0,8},{4,12},{8,0},{12,4},{1,9},{5,13},{9,1},{13,5},{2,10},{6,14},... | collective-permute-start | bytes 6291464 | tf_op jit(solution)/shard_map/cond/branch_2_fun/ppermute | solution.py:16
  5.6 0.9 reshape.79
  6.6 0.9 reshape.80
  7.5 0.1 dynamic-slice_bitcast_fusion.16
  7.6 0.2 concatenate.10
  7.8 23.7 %fusion.14 = f32[32,6144]{1,0:T(8,128)S(1)} fusion(bf16[32,3584]{1,0:T(8,128)(2,1)S(1)} %concatenate.10, bf16[448,8,48,128]{3,2,1,0:T(8,128)(2,1)} %bitcast.126), kind=kOutput, calls=%fused_computation.32 | convolution fusion | flops 1409286144 | bytes 45056000 | tf_op jit(solution)/shard_map/cond/branch_2_fun/dot_general | solution.py:170
  31.6 1.6 %collective-permute-start.8 = (bf16[2,8,6144]{2,1,0:T(8,128)(2,1)S(1)}, bf16[2,8,6144]{2,1,0:T(8,128)(2,1)S(1)}, u32[]{:S(2)}, u32[]{:S(2)}) collective-permute-start(bf16[2,8,6144]{2,1,0:T(8,128)(2,1)S(1)} %fusion.18), channel_id=1, source_target_pairs={{0,4},{4,0},{8,12},{12,8},{1,5},{5,1},{9,13},{13,9},{2,6},{6,2},{1... | collective-permute-start | bytes 589832 | tf_op jit(solution)/shard_map/cond/branch_2_fun/ppermute | solution.py:39
  33.2 21.8 %collective-permute-done.8 = bf16[2,8,6144]{2,1,0:T(8,128)(2,1)S(1)} collective-permute-done((bf16[2,8,6144]{2,1,0:T(8,128)(2,1)S(1)}, bf16[2,8,6144]{2,1,0:T(8,128)(2,1)S(1)}, u32[]{:S(2)}, u32[]{:S(2)}) %collective-permute-start.8) | collective-permute-done | bytes 196640 | tf_op jit(solution)/shard_map/cond/branch_2_fun/ppermute | solution.py:39
  55.1 2.4 %collective-permute-start.9 = (bf16[1,8,6144]{2,1,0:T(8,128)(2,1)S(1)}, bf16[1,8,6144]{2,1,0:T(8,128)(2,1)S(1)}, u32[]{:S(2)}, u32[]{:S(2)}) collective-permute-start(bf16[1,8,6144]{2,1,0:T(8,128)(2,1)S(1)} %slice.134), channel_id=1, source_target_pairs={{0,8},{4,12},{8,0},{12,4},{1,9},{5,13},{9,1},{13,5},{2,10},{6,14},... | collective-permute-start | bytes 294920 | tf_op jit(solution)/shard_map/cond/branch_2_fun/ppermute | solution.py:39
  57.5 43.1 %collective-permute-done.9 = bf16[1,8,6144]{2,1,0:T(8,128)(2,1)S(1)} collective-permute-done((bf16[1,8,6144]{2,1,0:T(8,128)(2,1)S(1)}, bf16[1,8,6144]{2,1,0:T(8,128)(2,1)S(1)}, u32[]{:S(2)}, u32[]{:S(2)}) %collective-permute-start.9) | collective-permute-done | bytes 98336 | tf_op jit(solution)/shard_map/cond/branch_2_fun/ppermute | solution.py:39
  100.7 0.0 collective-permute-done.7
  101.0 0.0 copy-done
  101.0 0.0 copy-done.1
  101.0 4.7 %attend.1 = (bf16[2,4,2048]{2,1,0:T(4,128)(2,1)}, bf16[4,64,2,16,128]{4,3,2,1,0:T(8,128)(2,1)}) custom-call(s32[16]{0:T(128)S(1)} %copy-done.1, s32[4]{0:T(128)S(1)} %copy-done, bf16[2,4,3,16,128]{4,3,2,1,0:T(8,128)(2,1)S(1)} %get-tuple-element.49.fresh_ref, bf16[4,64,2,16,128]{4,3,2,1,0:T(8,128)(2,1)} %cache_ref.1, ...), custom_call_target="tpu_custom_call" | custom-call | bytes 4194304 | tf_op jit(solution)/shard_map/attend/pallas_call | solution.py:128
  (5 shorter events, 0.1 us)
Async XLA Ops:
  1.3 99.7 %copy-start = (s32[4]{0:T(128)S(1)}, s32[4]{0:T(128)}, u32[]{:S(2)}) copy-start(s32[4]{0:T(128)} %matching_ref.1) | copy-start | bytes 52
  1.3 99.7 %copy-start.1 = (s32[16]{0:T(128)S(1)}, s32[16]{0:T(128)}, u32[]{:S(2)}) copy-start(s32[16]{0:T(128)} %lengths_ref.1) | copy-start | bytes 196
  1.5 99.2 %collective-permute-start.7 = (bf16[4,64,2,16,128]{4,3,2,1,0:T(8,128)(2,1)}, bf16[4,64,2,16,128]{4,3,2,1,0:T(8,128)(2,1)}, u32[]{:S(2)}, u32[]{:S(2)}) collective-permute-start(bf16[4,64,2,16,128]{4,3,2,1,0:T(8,128)(2,1)} %get-tuple-element.37), channel_id=1, source_target_pairs={{0,8},{4,12},{8,0},{12,4},{1,9},{5,13},{9,1},{13,5},{2,10},{6,14},... | collective-permute-start | bytes 6291464 | tf_op jit(solution)/shard_map/cond/branch_2_fun/ppermute | solution.py:16
  31.6 23.4 %collective-permute-start.8 = (bf16[2,8,6144]{2,1,0:T(8,128)(2,1)S(1)}, bf16[2,8,6144]{2,1,0:T(8,128)(2,1)S(1)}, u32[]{:S(2)}, u32[]{:S(2)}) collective-permute-start(bf16[2,8,6144]{2,1,0:T(8,128)(2,1)S(1)} %fusion.18), channel_id=1, source_target_pairs={{0,4},{4,0},{8,12},{12,8},{1,5},{5,1},{9,13},{13,9},{2,6},{6,2},{1... | collective-permute-start | bytes 589832 | tf_op jit(solution)/shard_map/cond/branch_2_fun/ppermute | solution.py:39
  55.1 45.6 %collective-permute-start.9 = (bf16[1,8,6144]{2,1,0:T(8,128)(2,1)S(1)}, bf16[1,8,6144]{2,1,0:T(8,128)(2,1)S(1)}, u32[]{:S(2)}, u32[]{:S(2)}) collective-permute-start(bf16[1,8,6144]{2,1,0:T(8,128)(2,1)S(1)} %slice.134), channel_id=1, source_target_pairs={{0,8},{4,12},{8,0},{12,4},{1,9},{5,13},{9,1},{13,5},{2,10},{6,14},... | collective-permute-start | bytes 294920 | tf_op jit(solution)/shard_map/cond/branch_2_fun/ppermute | solution.py:39
where the time goes:
time: 106 us
  waiting for transfers between devices  64.9 us (61%)
  matrix products  23.7 us (22%)
  starting transfers between devices  8.18 us (8%)
  Pallas kernels  4.71 us (4%)
  local copies, waits for them, and re-layouts  2.19 us (2%)
  between operations  1.54 us (1%)
    ppermute x2, waiting for transfers between devices, reduce_by_halves(): got = lax.ppermute(sent, 'tp', [(i, i ^ 1 << level) for i in range(owners)])  64.9 us
    dot_general x1, matrix products, serve(): jnp.dot(tokens, qkv_weight.reshape(qkv_weight.shape[0], -1), preferred_el...  23.7 us
    pallas_call x1, Pallas kernels, attend_and_write(): pl.pallas_call(attention_kernel, out_shape=(attended, jax.ShapeDtypeStruc...  4.71 us
    ppermute x1, starting transfers between devices, shifted(): lax.ppermute(block, axis, [(i, (i + by) % devices) for i in range(devices)])  4.1 us
    ppermute x2, starting transfers between devices, reduce_by_halves(): got = lax.ppermute(sent, 'tp', [(i, i ^ 1 << level) for i in range(owners)])  4.08 us
  transfers between devices with their start and end apart: 3, of which 2 were waited for; matrix products, arithmetic and copies ran while one was open for 25% of the time, Pallas kernels for 0%

commit v1 on v0

v1 whole, which is shorter than its diff:
```python
import functools
import math

import jax
import jax.numpy as jnp
from jax import lax
from jax.experimental import pallas as pl
from jax.experimental.pallas import tpu as pltpu
from jax.sharding import PartitionSpec as P

WIDEST_SWITCH = 8


def shifted(block, axis, by):
    devices = lax.axis_size(axis)
    return lax.ppermute(block, axis, [(i, (i + by) % devices) for i in range(devices)])


def rotate_by_bits(block, offset, owners):
    for level in range((owners - 1).bit_length()):
        moved = shifted(block, "tp", 1 << level)
        block = jnp.where(offset >> level & 1 == 1, moved, block)
    return block


def reduce_by_halves(parts, owners):
    distances = list(range(owners))
    blocks = [parts[distance] for distance in distances]
    stride = 1
    while stride < owners:
        kept = [i for i, distance in enumerate(distances) if not distance & stride]
        gone = [i for i, distance in enumerate(distances) if distance & stride]
        sent = jnp.stack([blocks[i] for i in gone]).astype(jnp.bfloat16)
        got = lax.ppermute(sent, "tp", [(i, i ^ stride) for i in range(owners)]).astype(jnp.float32)
        blocks = [blocks[i] + got[j] for j, i in enumerate(kept)]
        distances = [distances[i] for i in kept]
        stride *= 2
    return blocks[0]


def reduce_at_once(parts, owners):
    total = parts[0]
    for distance in range(1, owners):
        pairs = [(i, i ^ distance) for i in range(owners)]
        total = total + lax.ppermute(parts[distance].astype(jnp.bfloat16), "tp", pairs).astype(jnp.float32)
    return total


UNITS = 8
LENT_TO_BUSY, LENT_TO_IDLE = 2, 3


def slot_units():
    return {
        "whole": (0, UNITS),
        "most": (0, UNITS - LENT_TO_BUSY),
        "own": (UNITS - LENT_TO_BUSY, LENT_TO_BUSY),
        "lent": (UNITS - LENT_TO_BUSY, LENT_TO_BUSY),
        "more": (0, UNITS - LENT_TO_IDLE),
        "lent_more": (UNITS - LENT_TO_IDLE, LENT_TO_IDLE),
    }


def slot_is_mine(name, mine, other):
    moves, lends, helps = mine != 0, (mine == 2) & (other != 2), (mine != 2) & (other == 2)
    return {
        "whole": moves & jnp.logical_not(lends | helps),
        "most": moves & (other != 0) & (lends | helps),
        "own": moves & helps,
        "lent": lends & (other != 0),
        "more": lends & (other == 0),
        "lent_more": lends & (other == 0),
    }[name]


def attention_kernel(names, lengths_ref, matching_ref, other_ref, fresh_ref, cache_ref, *refs):
    slots = dict(zip(names, refs))
    attended_ref, filled_ref, block, mixed, result, load_sems, row_sems, token_sems, result_sem = refs[len(names) :]
    part, _, heads, head_dim = block.shape[1:]
    steps, rows = fresh_ref.shape[:2]
    per_row = UNITS // rows
    spots = per_row * part
    owners = lax.axis_size("tp")
    mine, other = matching_ref[0], other_ref[0]
    of_row = [block.at[pl.ds(r * per_row, per_row)] for r in range(rows)]
    arrivals = [pltpu.make_async_copy(cache_ref.at[pl.ds(r * per_row, per_row)], of_row[r], load_sems.at[r]) for r in range(rows)]
    stores = [pltpu.make_async_copy(of_row[r], filled_ref.at[pl.ds(r * per_row, per_row)], row_sems.at[r]) for r in range(rows)]

    def load(source, first, count):
        unit = first
        while unit < first + count:
            size = min(first + count, (unit // per_row + 1) * per_row) - unit
            pltpu.make_async_copy(
                source.at[pl.ds(unit - first, size)], block.at[pl.ds(unit, size)], load_sems.at[unit // per_row]
            ).start()
            unit += size

    @pl.when(mine == 0)
    def _():
        load(cache_ref, 0, UNITS)

    for name in names:

        @pl.when((mine != 0) if len(names) == 1 else slot_is_mine(name, mine, other))
        def _(name=name):
            load(slots[name], *slot_units()[name])

    first_row = lax.rem(lax.axis_index("tp") - matching_ref[0] + owners, owners) * rows
    first_head = lax.axis_index(("pp", "rep")) * heads
    level = heads.bit_length() - 1
    assert heads == 1 << level

    def relation(columns):
        shape = (steps * heads, columns * heads)
        row, column = (lax.broadcasted_iota(jnp.int32, shape, axis) for axis in range(2))
        head = (first_head + 1 + (row & (heads - 1))).astype(jnp.float32)
        slope = jnp.exp(head * (-math.log(2.0) / 8.0))
        return (row >> level) - (column >> level), (row ^ column) & (heads - 1) == 0, slope

    since, own, slope = relation(spots)
    bias = slope * since.astype(jnp.float32)
    place = lax.broadcasted_iota(jnp.int32, since.shape, 1) >> level
    place = jnp.where(own, place, spots)
    since, own, fresh_slope = relation(steps)
    fresh_bias = fresh_slope * since.astype(jnp.float32)
    fresh_allowed = own & (since >= 0)

    def scored(query, keys):
        scores = lax.dot_general(query, keys, (((1,), (1,)), ((), ())), preferred_element_type=jnp.float32)
        return scores * head_dim ** (-0.5)

    def weighed(weights, values):
        paired = jnp.concatenate([values, jnp.ones_like(values)], axis=1)
        return jnp.dot(weights.astype(values.dtype), paired, preferred_element_type=jnp.float32)

    for r in range(rows):
        arrivals[r].wait()
        stores[r].start()
    for r in range(rows):
        at = lengths_ref[first_row + r]
        query, fresh_keys, fresh_values = (
            fresh_ref[:, r, kind].reshape(steps * heads, head_dim) for kind in range(3)
        )
        before = scored(query, block[r * per_row : (r + 1) * per_row, :, 0].reshape(spots * heads, head_dim))
        before = before - (bias + slope * at.astype(jnp.float32))
        before = jnp.where(place < at, before, -1e30)
        fresh = jnp.where(fresh_allowed, scored(query, fresh_keys) - fresh_bias, -1e30)
        top = jnp.maximum(jnp.max(before, axis=1, keepdims=True), jnp.max(fresh, axis=1, keepdims=True))
        mix = weighed(jnp.exp(before - top), block[r * per_row : (r + 1) * per_row, :, 1].reshape(spots * heads, head_dim))
        mix = mix + weighed(jnp.exp(fresh - top), fresh_values)
        mixed[:, r] = (mix[:, :head_dim] / mix[:, head_dim:]).reshape(steps, heads, head_dim)
    tokens = []
    for r in range(rows):
        at = lengths_ref[first_row + r]
        stores[r].wait()
        for s in range(steps):
            unit, spot = r * per_row + lax.div(at + s, part), lax.rem(at + s, part)
            token = pltpu.make_async_copy(
                fresh_ref.at[s, r, pl.ds(1, 2)], filled_ref.at[unit, spot], token_sems.at[r, s]
            )
            token.start()
            tokens.append(token)
    for s in range(steps):
        for h in range(heads):
            result[s, :, h * head_dim : (h + 1) * head_dim] = mixed[s, :, h].astype(result.dtype)
    finish = pltpu.make_async_copy(result, attended_ref, result_sem)
    finish.start()
    for token in tokens:
        token.wait()
    finish.wait()


def unwritten(shape, dtype):
    return pl.pallas_call(
        lambda out_ref: None,
        out_shape=jax.ShapeDtypeStruct(shape, dtype),
        out_specs=pl.BlockSpec(memory_space=pl.ANY),
        name="unwritten",
    )()


def attend_and_write(units, slots, fresh, lengths, matching, other):
    steps, rows, _, heads, head_dim = fresh.shape
    smem, vmem = (pl.BlockSpec(memory_space=space) for space in (pltpu.SMEM, pltpu.VMEM))
    anywhere = pl.BlockSpec(memory_space=pl.ANY)
    attended = jax.ShapeDtypeStruct((steps, rows, heads * head_dim), jnp.bfloat16)
    return pl.pallas_call(
        functools.partial(attention_kernel, tuple(slots)),
        out_shape=(attended, jax.ShapeDtypeStruct(units.shape, units.dtype)),
        in_specs=[smem, smem, smem, vmem, anywhere] + [anywhere] * len(slots),
        out_specs=(anywhere, anywhere),
        scratch_shapes=[
            pltpu.VMEM(units.shape, units.dtype),
            pltpu.VMEM((steps, rows, heads, head_dim), jnp.float32),
            pltpu.VMEM(attended.shape, attended.dtype),
            pltpu.SemaphoreType.DMA((rows,)),
            pltpu.SemaphoreType.DMA((rows,)),
            pltpu.SemaphoreType.DMA((rows, steps)),
            pltpu.SemaphoreType.DMA,
        ],
        compiler_params=pltpu.CompilerParams(vmem_limit_bytes=32 << 20),
        cost_estimate=pl.CostEstimate(flops=0, bytes_accessed=4 * units.size, transcendentals=0),
        name="attend",
    )(lengths, matching, other, fresh, units, *slots.values())


def projection_kernel(piece, first_ref, second_ref, weight_ref, parts_ref, sums):
    step = pl.program_id(0)
    kinds, pairs, _, width = sums.shape
    owners, rows = parts_ref.shape[0], parts_ref.shape[3]

    @pl.when(step == 0)
    def _():
        sums[...] = jnp.zeros_like(sums)

    count = owners * rows
    to, source = (lax.broadcasted_iota(jnp.int32, (count, count), axis) for axis in range(2))
    local_rows = rows // 2
    block, token_step, row = lax.div(to, rows), lax.div(lax.rem(to, rows), local_rows), lax.rem(to, local_rows)
    owner = block ^ lax.axis_index("tp")
    picks = (token_step * owners + owner) * local_rows + row == source
    picks = jnp.where(picks, 1.0, 0.0).astype(first_ref.dtype)
    pieces = weight_ref.shape[0] // piece

    def add(index, carry):
        kind = lax.rem(index, kinds)
        depth = pl.ds(pl.multiple_of(lax.div(index, kinds) * piece, piece), piece) if pieces > 1 else slice(None)
        tokens = jnp.concatenate([first_ref[:, depth], second_ref[:, depth]])
        tokens = jnp.dot(picks, tokens, preferred_element_type=jnp.float32).astype(tokens.dtype)
        by_head = jnp.swapaxes(weight_ref[depth, kind], 0, 1)
        for pair in range(pairs):
            both = jnp.concatenate([by_head[2 * pair], by_head[2 * pair + 1]], axis=1)
            sums[kind, pair] += jnp.dot(tokens, both, preferred_element_type=jnp.float32)
        return carry

    lax.fori_loop(0, pieces * kinds, add, 0)

    @pl.when(step == pl.num_programs(0) - 1)
    def _():
        for distance in range(owners):
            parts_ref[distance] = sums[:, :, distance * rows : (distance + 1) * rows]


def largest_divisor(number, most, unit):
    return max(size for size in range(unit, most + 1, unit) if number % size == 0)


def multiply(first_tokens, second_tokens, weight, owners):
    depth, kinds, heads, head_dim = weight.shape
    block = largest_divisor(depth, 512, 64)
    piece = 256 if block % 256 == 0 else block
    requests = first_tokens.shape[0]
    sums = (kinds, heads // 2, 2 * requests, 2 * head_dim)
    parts = (owners, kinds, heads // 2, 2 * requests // owners, 2 * head_dim)
    return pl.pallas_call(
        functools.partial(projection_kernel, piece),
        out_shape=jax.ShapeDtypeStruct(parts, jnp.float32),
        grid=(depth // block,),
        in_specs=[
            pl.BlockSpec((requests, block), lambda step: (0, step)),
            pl.BlockSpec((requests, block), lambda step: (0, step)),
            pl.BlockSpec((block, kinds, heads, head_dim), lambda step: (step, 0, 0, 0)),
        ],
        out_specs=pl.BlockSpec(parts, lambda step: (0,) * len(parts)),
        scratch_shapes=[pltpu.VMEM(sums, jnp.float32)],
        compiler_params=pltpu.CompilerParams(vmem_limit_bytes=48 << 20),
        cost_estimate=pl.CostEstimate(
            flops=4 * requests * weight.size, bytes_accessed=2 * weight.size, transcendentals=0
        ),
        name="project",
    )(first_tokens, second_tokens, weight)


def move_alone(units, by, owners):
    return {"whole": shifted(units, "tp", by)} if by else {}


def move_helped(units, heavy, by, owners):
    light = 1 - heavy

    def send(block, pairs):
        return lax.ppermute(block, ("grp", "tp"), pairs)

    def at(group, owner):
        return group * owners + owner % owners

    own = [(at(light, t), at(light, t + by)) for t in range(owners) if by]
    direct = [(at(heavy, t), at(heavy, t + 2)) for t in range(owners)] + own
    over = [(at(heavy, t), at(light, t)) for t in range(owners)]
    back = [(at(light, t), at(heavy, t + 2)) for t in range(owners)]
    split = UNITS - (LENT_TO_BUSY if by else LENT_TO_IDLE)
    most, last = units[:split], units[split:]
    lent = send(send(last, over), back)
    if by:
        return {"most": send(most, direct), "own": send(last, own), "lent": lent}
    return {"more": send(most, direct), "lent_more": lent}


def shards(first_tokens, second_tokens, qkv_weight, cache, lengths, matching):
    owners, groups = lax.axis_size("tp"), lax.axis_size("grp")
    assert owners & (owners - 1) == 0
    local_rows = cache.shape[0]
    heads_local = qkv_weight.shape[2]
    head_dim = qkv_weight.shape[3]
    units = cache.reshape(UNITS, -1, *cache.shape[2:])
    mine = matching[:1]

    def finish(fresh, slots, other):
        attended, filled = attend_and_write(units, slots, fresh, lengths, matching, other)
        return attended, filled.reshape(cache.shape)

    def project(reduce, first_tokens, second_tokens, qkv_weight):
        total = reduce(multiply(first_tokens, second_tokens, qkv_weight, owners), owners)
        fresh = total.astype(jnp.bfloat16).reshape(3, heads_local // 2, 2, local_rows, 2, head_dim)
        return fresh.transpose(2, 3, 0, 1, 4, 5).reshape(2, local_rows, 3, heads_local, head_dim)

    if owners > WIDEST_SWITCH:
        slots = {"whole": rotate_by_bits(units, matching[0], owners)}
        return finish(project(reduce_by_halves, first_tokens, second_tokens, qkv_weight), slots, mine)

    helps = owners == 4 and groups == 2
    names = slot_units() if helps else {"whole": slot_units()["whole"]}

    def branch(move, busy, first_tokens, second_tokens, qkv_weight, units):
        slots = move(units)
        fresh = project(reduce_by_halves if busy else reduce_at_once, first_tokens, second_tokens, qkv_weight)
        filled = {
            name: slots[name] if name in slots else unwritten((count, *units.shape[1:]), units.dtype)
            for name, (_, count) in names.items()
        }
        return fresh, filled

    plans = [(functools.partial(move_alone, by=by, owners=owners), min(by, owners - by) > 1) for by in range(owners)]
    other, index = mine, jnp.clip(matching[0], 0, owners - 1)
    if helps:
        light_offsets = (0, 1, 3)
        plans += [
            (functools.partial(move_helped, heavy=heavy, by=by, owners=owners), by != 0)
            for heavy in range(2)
            for by in light_offsets
        ]
        other = lax.ppermute(mine, "grp", [(0, 1), (1, 0)])
        group, offset = lax.axis_index("grp"), index
        lends = sum((owners + 3 * group + i) << 4 * by for i, by in enumerate(light_offsets)) + (2 << 8)
        helped = (owners + 3 * (1 - group) + ((offset + 1) >> 1)) << 8
        alone = sum(offset << 4 * by for by in light_offsets)
        table = jnp.where(offset == 2, lends, alone + helped)
        index = (table >> (4 * other[0])) & 15
    branches = [functools.partial(branch, move, busy) for move, busy in plans]
    fresh, slots = lax.switch(index, branches, first_tokens, second_tokens, qkv_weight, units)
    return finish(fresh, slots, other)


def solution(mesh):
    in_specs = (
        P("grp", "tp"),
        P("grp", "tp"),
        P("tp", None, ("pp", "rep"), None),
        P(("grp", "tp"), None, None, ("pp", "rep"), None),
        P("grp"),
        P("grp"),
    )
    out_specs = (
        P(None, ("grp", "tp"), ("pp", "rep")),
        P(("grp", "tp"), None, None, ("pp", "rep"), None),
    )
    return jax.shard_map(shards, mesh=mesh, in_specs=in_specs, out_specs=out_specs, check_vma=False)
```

time: 106 us -> 68.2 us (0.64)
  the two profiles are of different devices: /device:TPU:0 before, /device:TPU:29 now
where the time goes in v1:
time: 68.2 us; the launch traced here: 67.8 us
  waiting for transfers between devices  31.2 us (46%)
  Pallas kernels  29.7 us (44%)
  starting transfers between devices  3.96 us (6%)
  between operations  2 us (3%)
  local copies, waits for them, and re-layouts  0.78 us (1%)
    ppermute x3, waiting for transfers between devices, reduce_at_once(): lax.ppermute(parts[distance].astype(jnp.bfloat16), 'tp', pairs)  29.6 us
    pallas_call x1, Pallas kernels, multiply(): pl.pallas_call(functools.partial(projection_kernel, piece), out_shape=jax...  24.7 us
    pallas_call x1, Pallas kernels, attend_and_write(): pl.pallas_call(functools.partial(attention_kernel, tuple(slots)), out_sha...  5 us
    ppermute x3, starting transfers between devices, reduce_at_once(): lax.ppermute(parts[distance].astype(jnp.bfloat16), 'tp', pairs)  3.45 us
    ppermute x1, waiting for transfers between devices, shards(): other = lax.ppermute(mine, 'grp', [(0, 1), (1, 0)])  1.55 us
  transfers between devices with their start and end apart: 5, of which 3 were waited for; matrix products, arithmetic and copies ran while one was open for 1% of the time, Pallas kernels for 36%

profile of v1, /device:TPU:29, one launch (start us, length us, event | category | flops | bytes accessed | tf_op | source)
XLA Modules:
  0.0 67.8 jit_solution(4134099136423302411)
XLA Ops:
  0.6 0.3 collective-permute-start.50
  1.6 1.6 %collective-permute-done.50.other_ref = s32[1]{0:T(128)} collective-permute-done((s32[1]{0:T(128)}, s32[1]{0:T(128)}, u32[]{:S(2)}, u32[]{:S(2)}) %collective-permute-start.50) | collective-permute-done | bytes 36 | tf_op jit(solution)/shard_map/ppermute | solution.py:342
  3.8 0.0 copy-start
  3.8 0.0 copy-start.1
  3.8 58.9 %conditional.1 = (bf16[2,4,3,16,128]{4,3,2,1,0:T(8,128)(2,1)}, bf16[2,32,2,16,128]{4,3,2,1,0:T(8,128)(2,1)}, bf16[3,32,2,16,128]{4,3,2,1,0:T(8,128)(2,1)}, bf16[...) conditional(s32[]{:T(128)} %clamp.3, ...), branch_computations={%region_0.1_spmd, %region_1.2_spmd, %region_2.3_spmd, %region_3.4_... | conditional | flops 1409974272 | bytes 66945376 | solution.py:350
  3.9 0.2 collective-permute-start.10
  4.1 24.7 %project.13 = f32[4,3,8,8,256]{4,3,2,1,0:T(8,128)S(1)} custom-call(bf16[16,3584]{1,0:T(8,128)(2,1)} %get-tuple-element.89.first_ref, bf16[16,3584]{1,0:T(8,128)(2,1)} %get-tuple-element.90.second_ref, bf16[3584,3,16,128]{3,2,1,0:T(8,128)(2,1)} %get-tuple-element.91.weight_ref), custom_call_target="tpu_custom_call" | custom-call | flops 1409286144 | bytes 44040192 | tf_op jit(solution)/shard_map/cond/branch_3_fun/project/pallas_call | solution.py:255
  28.9 0.2 collective-permute-start.7
  29.1 3.0 %collective-permute-start.9 = (bf16[3,8,8,256]{3,2,1,0:T(8,128)(2,1)S(1)}, bf16[3,8,8,256]{3,2,1,0:T(8,128)(2,1)S(1)}, u32[]{:S(2)}, u32[]{:S(2)}) collective-permute-start(bf16[3,8,8,256]{3,2,1,0:T(8,128)(2,1)S(1)} %get-tuple-element.146), channel_id=1, source_target_pairs={{0,12},{4,8},{8,4},{12,0},{1,13},{5,9},{9,5},{13,1},{2,14},{6,10},... | collective-permute-start | bytes 294920 | tf_op jit(solution)/shard_map/cond/branch_3_fun/ppermute | solution.py:45
  32.1 0.2 collective-permute-start.8
  32.3 24.3 %collective-permute-done.7 = bf16[3,8,8,256]{3,2,1,0:T(8,128)(2,1)S(1)} collective-permute-done((bf16[3,8,8,256]{3,2,1,0:T(8,128)(2,1)S(1)}, bf16[3,8,8,256]{3,2,1,0:T(8,128)(2,1)S(1)}, u32[]{:S(2)}, u32[]{:S(2)}) %collective-permute-start.7) | collective-permute-done | bytes 98336 | tf_op jit(solution)/shard_map/cond/branch_3_fun/ppermute | solution.py:45
  56.6 0.0 collective-permute-done.9
  56.6 5.4 %collective-permute-done.8 = bf16[3,8,8,256]{3,2,1,0:T(8,128)(2,1)S(1)} collective-permute-done((bf16[3,8,8,256]{3,2,1,0:T(8,128)(2,1)S(1)}, bf16[3,8,8,256]{3,2,1,0:T(8,128)(2,1)S(1)}, u32[]{:S(2)}, u32[]{:S(2)}) %collective-permute-start.8) | collective-permute-done | bytes 98336 | tf_op jit(solution)/shard_map/cond/branch_3_fun/ppermute | solution.py:45
  62.0 0.7 %copy.11 = bf16[2,4,3,8,2,128]{5,4,3,2,1,0:T(2,128)(2,1)} copy(bf16[2,4,3,8,2,128]{5,4,1,0,3,2:T(2,128)(2,1)S(1)} %bitcast.142) | data formatting | bytes 196608 | tf_op jit(solution)/shard_map/cond/branch_3_fun/transpose | solution.py:315
  62.8 0.0 collective-permute-done.10
  62.8 0.0 copy-done
  62.8 0.0 copy-done.1
  62.8 5.0 %attend.1 = (bf16[2,4,2048]{2,1,0:T(4,128)(2,1)}, bf16[8,32,2,16,128]{4,3,2,1,0:T(8,128)(2,1)}) custom-call(s32[16]{0:T(128)S(1)} %copy-done, s32[4]{0:T(128)S(1)} %copy-done.1, s32[1]{0:T(128)} %collective-permute-done.50.other_ref, bf16[2,4,3,16,128]{4,3,2,1,0:T(8,128)(2,1)} %get-tuple-element.128.fresh_ref, bf16[8,32,2,16,128]{4,3,2,1,0:T(8,128)(2,1)} %bitcast.138, ...), custom_call_target="tpu_custom_call" | custom-call | bytes 4194304 | tf_op jit(solution)/shard_map/attend/pallas_call | solution.py:187
  (9 shorter events, 0.1 us)
Async XLA Ops:
  0.6 2.5 %collective-permute-start.50 = (s32[1]{0:T(128)}, s32[1]{0:T(128)}, u32[]{:S(2)}, u32[]{:S(2)}) collective-permute-start(s32[1]{0:T(128)} %bitcast.127), channel_id=1, source_target_pairs={{0,16},{16,0},{1,17},{17,1},{2,18},{18,2},{3,19},{19,3},{4,20},{20... | collective-permute-start | bytes 20 | tf_op jit(solution)/shard_map/ppermute | solution.py:342
  3.8 58.9 %copy-start = (s32[16]{0:T(128)S(1)}, s32[16]{0:T(128)}, u32[]{:S(2)}) copy-start(s32[16]{0:T(128)} %lengths_ref.1) | copy-start | bytes 196
  3.8 58.9 %copy-start.1 = (s32[4]{0:T(128)S(1)}, s32[4]{0:T(128)}, u32[]{:S(2)}) copy-start(s32[4]{0:T(128)} %matching_ref.1) | copy-start | bytes 52
  3.9 58.9 %collective-permute-start.10 = (bf16[8,32,2,16,128]{4,3,2,1,0:T(8,128)(2,1)}, bf16[8,32,2,16,128]{4,3,2,1,0:T(8,128)(2,1)}, u32[]{:S(2)}, u32[]{:S(2)}) collective-permute-start(bf16[8,32,2,16,128]{4,3,2,1,0:T(8,128)(2,1)} %get-tuple-element.92), channel_id=1, source_target_pairs={{0,12},{4,0},{8,4},{12,8},{1,13},{5,1},{9,5},{13,9},{2,14},{6,2},{... | collective-permute-start | bytes 6291464 | tf_op jit(solution)/shard_map/cond/branch_3_fun/ppermute | solution.py:16
  28.9 27.7 %collective-permute-start.7 = (bf16[3,8,8,256]{3,2,1,0:T(8,128)(2,1)S(1)}, bf16[3,8,8,256]{3,2,1,0:T(8,128)(2,1)S(1)}, u32[]{:S(2)}, u32[]{:S(2)}) collective-permute-start(bf16[3,8,8,256]{3,2,1,0:T(8,128)(2,1)S(1)} %get-tuple-element.145), channel_id=1, source_target_pairs={{0,4},{4,0},{8,12},{12,8},{1,5},{5,1},{9,13},{13,9},{2,6},{6,2},{1... | collective-permute-start | bytes 294920 | tf_op jit(solution)/shard_map/cond/branch_3_fun/ppermute | solution.py:45
  29.1 27.5 %collective-permute-start.9 = (bf16[3,8,8,256]{3,2,1,0:T(8,128)(2,1)S(1)}, bf16[3,8,8,256]{3,2,1,0:T(8,128)(2,1)S(1)}, u32[]{:S(2)}, u32[]{:S(2)}) collective-permute-start(bf16[3,8,8,256]{3,2,1,0:T(8,128)(2,1)S(1)} %get-tuple-element.146), channel_id=1, source_target_pairs={{0,12},{4,8},{8,4},{12,0},{1,13},{5,9},{9,5},{13,1},{2,14},{6,10},... | collective-permute-start | bytes 294920 | tf_op jit(solution)/shard_map/cond/branch_3_fun/ppermute | solution.py:45
  32.1 29.8 %collective-permute-start.8 = (bf16[3,8,8,256]{3,2,1,0:T(8,128)(2,1)S(1)}, bf16[3,8,8,256]{3,2,1,0:T(8,128)(2,1)S(1)}, u32[]{:S(2)}, u32[]{:S(2)}) collective-permute-start(bf16[3,8,8,256]{3,2,1,0:T(8,128)(2,1)S(1)} %get-tuple-element.147), channel_id=1, source_target_pairs={{0,8},{4,12},{8,0},{12,4},{1,9},{5,13},{9,1},{13,5},{2,10},{6,14},... | collective-permute-start | bytes 294920 | tf_op jit(solution)/shard_map/cond/branch_3_fun/ppermute | solution.py:45
